TPU v7x, 32 devices: a whole 2x2x4 slice. The times are simulated.
32 devices in a mesh: section: 8 (over z, x), tensor: 4 (over y, core).
Axes of the slice: x: 2, y: 2, z: 4, core: 2. Of those that a mesh axis runs over, the one named last changes fastest.
Arguments:
- state: bfloat16 [8, 16, 2560], P('section'), may hold values from -6 to 6
- gain_in: bfloat16 [8, 2560], P('section'), may hold values from 0.25 to 1.75
- w_query: bfloat16 [8, 2560, 4096], P('section', None, 'tensor'), may hold values from -0.125 to 0.125
- w_key: bfloat16 [8, 2560, 512], P('section', None, 'tensor'), may hold values from -0.125 to 0.125
- w_value: bfloat16 [8, 2560, 512], P('section', None, 'tensor'), may hold values from -0.125 to 0.125
- w_output: bfloat16 [8, 4096, 2560], P('section', 'tensor'), may hold values from -0.375 to 0.375
- query_gain: bfloat16 [8, 128], P('section'), may hold values from 0.099609375 to 1.8984375
- key_gain: bfloat16 [8, 128], P('section'), may hold values from 0.099609375 to 1.8984375
- cache_keys: bfloat16 [8, 16, 4, 32, 128], P('section', None, 'tensor'), may hold values from -600 to 600
- cache_values: bfloat16 [8, 16, 4, 32, 128], P('section', None, 'tensor'), may hold values from -6 to 6
- lengths: int32 [8, 16], P('section'), may hold values from 4 to 32, as said below
Outputs:
- handed: bfloat16 [8, 16, 2560], P('section')
- new_keys: bfloat16 [8, 16, 4, 128], P('section', None, 'tensor')
- new_values: bfloat16 [8, 16, 4, 128], P('section', None, 'tensor')
Inputs may be any that keep to these rules, and one draw needn't show every extreme that they name: `lengths`: in every section at least one row holds 32 tokens.
All inputs are finite; a program needn't handle non-finite values.
Results may differ from a plain program's by a relative error of at most 0.012.
The roundings to bfloat16 on the way count: a program that leaves them out, or rounds other values in their place, can miss the bound.
Values may be sent and summed in bfloat16 or wider, within the bound.
A program may use at most 64 MiB of HBM per device.

v0:
```python
import jax
import jax.numpy as jnp
from jax import lax
from jax.sharding import PartitionSpec as P

HD = 128


epsilon = 1e-06
rope_base = 1000000.0


def shifted(value, axis, steps):
    count = lax.axis_size(axis)
    pairs = [(source, (source + steps) % count) for source in range(count)]
    return lax.ppermute(value, axis, pairs)


def rms_norm(values, gain_vec):
    return (
        values
        * lax.rsqrt(jnp.mean(values * values, axis=-1, keepdims=True) + epsilon)
        * gain_vec.astype(jnp.float32)
    )


def rotate(values, position):
    half_dim = values.shape[-1] // 2
    frequency = rope_base ** (-(jnp.arange(half_dim, dtype=jnp.float32) * 2.0 / values.shape[-1]))
    angles = position.astype(jnp.float32)[:, None] * frequency[None, :]
    target_shape = (angles.shape[0],) + (1,) * (values.ndim - 2) + (half_dim,)
    cosine = jnp.cos(angles).reshape(target_shape)
    sine = jnp.sin(angles).reshape(target_shape)
    lower_half = values[..., :half_dim]
    upper_half = values[..., half_dim:]
    return jnp.concatenate(
        [lower_half * cosine - upper_half * sine, upper_half * cosine + lower_half * sine], axis=-1
    )


def attend(
    hidden_in, gain_in, w_query, w_key, w_value, query_gain, key_gain, cache_key, cache_val, lengths
):
    row_count = hidden_in.shape[0]
    kv_heads = w_key.shape[1] // HD
    head_group = w_query.shape[1] // w_key.shape[1]
    normed = rms_norm(hidden_in.astype(jnp.float32), gain_in).astype(jnp.bfloat16)
    query = jnp.dot(normed, w_query, preferred_element_type=jnp.float32).reshape(
        row_count, kv_heads, head_group, HD
    )
    key_raw = jnp.dot(normed, w_key, preferred_element_type=jnp.float32).reshape(
        row_count, kv_heads, HD
    )
    new_value = (
        jnp.dot(normed, w_value, preferred_element_type=jnp.float32)
        .astype(jnp.bfloat16)
        .reshape(row_count, kv_heads, HD)
    )
    query_rot = rotate(rms_norm(query, query_gain), lengths).astype(jnp.bfloat16)
    new_key = rotate(rms_norm(key_raw, key_gain), lengths).astype(jnp.bfloat16)
    score_scale = HD ** (-0.5)
    cache_score = (
        jnp.einsum("rkgd,rkjd->rkgj", query_rot, cache_key, preferred_element_type=jnp.float32)
        * score_scale
    )
    own_score = (
        jnp.einsum("rkgd,rkd->rkg", query_rot, new_key, preferred_element_type=jnp.float32)
        * score_scale
    )
    in_cache = jnp.arange(cache_key.shape[2])[None, None, None, :] < lengths[:, None, None, None]
    masked = jnp.where(in_cache, cache_score, -1e30)
    row_max = jnp.maximum(jnp.max(masked, axis=-1), own_score)
    cache_exp = jnp.where(in_cache, jnp.exp(masked - row_max[..., None]), 0.0)
    own_exp = jnp.exp(own_score - row_max)
    denom_sum = jnp.sum(cache_exp, axis=-1) + own_exp
    cache_prob = (cache_exp / denom_sum[..., None]).astype(jnp.bfloat16)
    own_prob = (own_exp / denom_sum).astype(jnp.bfloat16)
    attended = jnp.einsum(
        "rkgj,rkjd->rkgd", cache_prob, cache_val, preferred_element_type=jnp.float32
    )
    attended = (
        attended
        + own_prob.astype(jnp.float32)[..., None] * new_value.astype(jnp.float32)[:, :, None, :]
    )
    attended = attended.astype(jnp.bfloat16).reshape(row_count, kv_heads * head_group * HD)
    return (attended, new_key, new_value)


def body(
    state,
    gain_in,
    w_query,
    w_key,
    w_value,
    w_output,
    query_gain,
    key_gain,
    cache_keys,
    cache_values,
    lengths,
):
    hidden_in = state[0]
    projection = w_output[0]
    attended, new_key, new_value = attend(
        hidden_in,
        gain_in[0],
        w_query[0],
        w_key[0],
        w_value[0],
        query_gain[0],
        key_gain[0],
        cache_keys[0],
        cache_values[0],
        lengths[0],
    )
    partial_value = jnp.dot(attended, projection, preferred_element_type=jnp.float32)
    summed = lax.psum(partial_value, "tensor")
    result = (hidden_in.astype(jnp.float32) + summed).astype(jnp.bfloat16)
    handed = shifted(result, "section", 1)
    return (handed[None], new_key[None], new_value[None])


def solution(mesh):
    placed = (
        P("section", None, None),
        P("section", None),
        P("section", None, "tensor"),
        P("section", None, "tensor"),
        P("section", None, "tensor"),
        P("section", "tensor", None),
        P("section", None),
        P("section", None),
        P("section", None, "tensor", None, None),
        P("section", None, "tensor", None, None),
        P("section", None),
    )
    return jax.shard_map(
        body,
        mesh=mesh,
        in_specs=placed,
        out_specs=(
            P("section", None, None),
            P("section", None, "tensor", None),
            P("section", None, "tensor", None),
        ),
        check_vma=False,
    )
```

profile of v0, /device:TPU:0, one launch (start us, length us, event | category | flops | bytes accessed | tf_op | source)
XLA Modules:
  0.0 72.2 jit_solution(17608033250856012103)
XLA Ops:
  7.2 0.0 copy-start
  7.2 0.0 copy-start.3
  7.2 0.0 copy-start.4
  7.2 0.0 all-reduce.2.cloned.1.call-start
  7.2 0.0 copy-start.1
  7.3 0.8 %bitcast_convert_fusion.2 = f32[16]{0:T(128)S(1)} fusion(s32[1,16]{1,0:T(1,128)} %param.21), kind=kLoop, calls=%fused_computation.73 | loop fusion | flops 16 | bytes 128 | tf_op jit(solution)/shard_map/convert_element_type | solution.py:30
  8.1 1.1 %bitcast_convert_fusion.1 = f32[128]{0:T(128)S(1)} fusion(bf16[1,128]{1,0:T(2,128)(2,1)} %param.17), kind=kLoop, calls=%fused_computation.67 | loop fusion | flops 128 | bytes 768 | tf_op jit(solution)/shard_map/convert_element_type | solution.py:23
  9.2 0.7 bitcast_convert_fusion
  9.8 1.0 %fusion.14 = f32[16]{0:T(128)S(1)} fusion(bf16[1,16,2560]{2,1,0:T(8,128)(2,1)} %param.11), kind=kLoop, calls=%fused_computation.17 | loop fusion | flops 122864 | bytes 81984 | tf_op jit(solution)/shard_map/reduce_sum | solution.py:22
  10.8 0.7 %iota_compare_fusion = pred[16,32]{1,0:T(8,128)(4,1)S(1)} fusion(s32[16]{0:T(128)} %bitcast.89), kind=kLoop, calls=%fused_computation.58 | loop fusion | flops 512 | bytes 576 | tf_op jit(solution)/shard_map/lt | solution.py:70
  11.6 0.7 %convert_reduce_fusion = f32[2560]{0:T(1024)S(1)} fusion(bf16[1,2560]{1,0:T(2,128)(2,1)} %param.12), kind=kLoop, calls=%fused_computation.48 | loop fusion | flops 2560 | bytes 15360 | tf_op jit(solution)/shard_map/mul | solution.py:21
  12.3 1.5 %multiply_reduce_fusion.1 = (f32[16]{0:T(128)S(1)}, f32[16,128]{1,0:T(8,128)S(1)}) fusion(bf16[1,2560,128]{2,1,0:T(8,128)(2,1)} %param.14, bf16[1,16,2560]{2,1,0:T(8,128)(2,1)} %param.11, f32[2560]{0:T(1024)S(1)} %convert_reduce_fusion, f32[16]{0:T(128)S(1)} %add_rsqrt_fusion.2), kind=kOutput, calls=%fused_computation.56 | convolution fusion | flops 10653680 | bytes 755840 | tf_op jit(solution)/shard_map/dot_general | solution.py:51
  13.8 0.1 multiply_cosine_fusion.1
  14.0 0.1 multiply_bitcast_fusion
  14.0 0.1 fusion.35
  14.2 0.0 copy-done
  14.2 1.7 %fusion.48 = (f32[16,128]{1,0:T(8,128)S(1)}, bf16[16,128]{1,0:T(8,128)(2,1)}) fusion(bf16[1,2560,128]{2,1,0:T(8,128)(2,1)S(1)} %copy-done, bf16[1,16,2560]{2,1,0:T(8,128)(2,1)} %param.11, f32[2560]{0:T(1024)S(1)} %convert_reduce_fusion, f32[16]{0:T(128)S(1)} %add_rsqrt_fusion.2), kind=kOutput, calls=%fused_computation.75 | convolution fusion | flops 10653696 | bytes 759872 | tf_op jit(solution)/shard_map/dot_general | solution.py:55
  15.9 0.0 copy-start.2
  15.9 3.4 %fusion.4 = f32[2,8,8,128]{3,1,2,0:T(8,128)S(1)} fusion(bf16[1,2560,1024]{2,1,0:T(8,128)(2,1)} %param.13, bf16[1,16,2560]{2,1,0:T(8,128)(2,1)} %param.11, f32[2560]{0:T(1024)S(1)} %convert_reduce_fusion, f32[16]{0:T(128)S(1)} %add_rsqrt_fusion.2), kind=kOutput, calls=%fused_computation.4 | convolution fusion | flops 84049920 | bytes 5400640 | tf_op jit(solution)/shard_map/dot_general | solution.py:48
  19.3 0.1 multiply_reduce_fusion
  19.4 0.1 maximum_bitcast_fusion
  19.5 0.1 multiply_multiply_fusion
  19.6 0.1 fusion.22
  19.7 0.2 fusion.38
  19.9 0.0 copy-done.3
  19.9 0.3 fusion.49
  20.2 0.2 fusion.21
  20.5 0.0 copy-done.4
  20.5 0.2 fusion.8
  20.7 0.0 copy-done.1
  20.7 1.5 %fusion = f32[16,2560]{1,0:T(8,128)} fusion(bf16[1,1024,2560]{2,1,0:T(8,128)(2,1)S(1)} %copy-done.1, bf16[2,8,8,128]{3,2,1,0:T(8,128)(2,1)S(1)} %bitcast.85), kind=kOutput, calls=%fused_computation | convolution fusion | flops 83886080 | bytes 5439488 | tf_op jit(solution)/shard_map/dot_general | solution.py:116
  22.2 0.0 all-reduce.2.cloned.1.call-update
  22.2 34.4 %all-reduce.2.cloned.1.call-done = f32[16,2560]{1,0:T(8,128)} async-done(((f32[16,2560]{1,0:T(8,128)}), f32[16,2560]{1,0:T(8,128)}) %all-reduce.2.cloned.1.call-update) | async-done | bytes 163856 | tf_op jit(solution)/shard_map/psum | solution.py:117
  56.6 0.0 copy-done.2
  56.6 0.9 %fusion.15 = bf16[16,2560]{1,0:T(8,128)(2,1)S(1)} fusion(f32[16,2560]{1,0:T(8,128)} %all-reduce.2.cloned.1.call-done, bf16[1,16,2560]{2,1,0:T(8,128)(2,1)S(1)} %copy-done.2), kind=kLoop, calls=%fused_computation.18 | loop fusion | flops 122880 | bytes 327680 | tf_op jit(solution)/shard_map/convert_element_type | solution.py:118
  57.6 1.5 %collective-permute-start = (bf16[16,2560]{1,0:T(8,128)(2,1)S(1)}, bf16[16,2560]{1,0:T(8,128)(2,1)S(1)}, u32[]{:S(2)}, u32[]{:S(2)}) collective-permute-start(bf16[16,2560]{1,0:T(8,128)(2,1)S(1)} %fusion.15), channel_id=1, source_target_pairs={{0,4},{4,8},{8,12},{12,16},{16,20},{20,24},{24,28},{28,0},{1,5},{5... | collective-permute-start | bytes 245768 | tf_op jit(solution)/shard_map/ppermute | solution.py:16
  59.1 0.7 pad_maximum_fusion.3
  59.7 5.0 %collective-permute-done = bf16[16,2560]{1,0:T(8,128)(2,1)S(1)} collective-permute-done((bf16[16,2560]{1,0:T(8,128)(2,1)S(1)}, bf16[16,2560]{1,0:T(8,128)(2,1)S(1)}, u32[]{:S(2)}, u32[]{:S(2)}) %collective-permute-start) | collective-permute-done | bytes 81952 | tf_op jit(solution)/shard_map/ppermute | solution.py:16
  64.7 0.6 copy.26
  (7 shorter events, 0.1 us)
Async XLA Ops:
  7.2 7.0 %copy-start = (bf16[1,2560,128]{2,1,0:T(8,128)(2,1)S(1)}, bf16[1,2560,128]{2,1,0:T(8,128)(2,1)}, u32[]{:S(2)}) copy-start(bf16[1,2560,128]{2,1,0:T(8,128)(2,1)} %param.15) | copy-start | bytes 1966084
  7.2 12.7 %copy-start.3 = (bf16[1,16,1,32,128]{4,3,2,1,0:T(8,128)(2,1)S(1)}, bf16[1,16,1,32,128]{4,3,2,1,0:T(8,128)(2,1)}, u32[]{:S(2)}) copy-start(bf16[1,16,1,32,128]{4,3,2,1,0:T(8,128)(2,1)} %param.19) | copy-start | bytes 393220
  7.2 13.3 %copy-start.4 = (bf16[1,16,1,32,128]{4,3,2,1,0:T(8,128)(2,1)S(1)}, bf16[1,16,1,32,128]{4,3,2,1,0:T(8,128)(2,1)}, u32[]{:S(2)}) copy-start(bf16[1,16,1,32,128]{4,3,2,1,0:T(8,128)(2,1)} %param.20) | copy-start | bytes 393220
  7.2 49.4 %all-reduce.2.cloned.1.call-start = ((), (), s32[]{:S(2)}) async-start(), calls=%async_computation | async-start | bytes 327680 | tf_op jit(solution)/shard_map/psum | solution.py:117
  7.2 13.5 %copy-start.1 = (bf16[1,1024,2560]{2,1,0:T(8,128)(2,1)S(1)}, bf16[1,1024,2560]{2,1,0:T(8,128)(2,1)}, u32[]{:S(2)}) copy-start(bf16[1,1024,2560]{2,1,0:T(8,128)(2,1)} %param.16) | copy-start | bytes 15728644
  15.9 40.7 %copy-start.2 = (bf16[1,16,2560]{2,1,0:T(8,128)(2,1)S(1)}, bf16[1,16,2560]{2,1,0:T(8,128)(2,1)}, u32[]{:S(2)}) copy-start(bf16[1,16,2560]{2,1,0:T(8,128)(2,1)} %param.11) | copy-start | bytes 245764
  57.6 7.2 %collective-permute-start = (bf16[16,2560]{1,0:T(8,128)(2,1)S(1)}, bf16[16,2560]{1,0:T(8,128)(2,1)S(1)}, u32[]{:S(2)}, u32[]{:S(2)}) collective-permute-start(bf16[16,2560]{1,0:T(8,128)(2,1)S(1)} %fusion.15), channel_id=1, source_target_pairs={{0,4},{4,8},{8,12},{12,16},{16,20},{20,24},{24,28},{28,0},{1,5},{5... | collective-permute-start | bytes 245768 | tf_op jit(solution)/shard_map/ppermute | solution.py:16
Sparse Core Ops, SparseCore 0:
  22.3 34.2 all-reduce.1
where the time goes:
time: 72.5 us; the launch traced here: 72.2 us
  waiting for transfers between devices  39.5 us (54%)
  between operations  14.2 us (20%)
  matrix products  8.84 us (12%)
  other arithmetic  7.52 us (10%)
  starting transfers between devices  1.56 us (2%)
    psum x1, waiting for transfers between devices, body(): summed = lax.psum(partial_value, 'tensor')  34.4 us
    ppermute x1, waiting for transfers between devices, shifted(): return lax.ppermute(value, axis, pairs)  5 us
    dot_general x1, matrix products, attend(): jnp.dot(normed, w_query, preferred_element_type=jnp.float32)  3.39 us
    dot_general x1, matrix products, attend(): jnp.dot(normed, w_value, preferred_element_type=jnp.float32)  1.75 us
    convert_element_type x2, other arithmetic, rms_norm(): gain_vec.astype(jnp.float32)  1.73 us
    ppermute x1, starting transfers between devices, shifted(): return lax.ppermute(value, axis, pairs)  1.52 us
    dot_general x1, matrix products, attend(): jnp.dot(normed, w_key, preferred_element_type=jnp.float32)  1.5 us
    dot_general x1, matrix products, body(): jnp.dot(attended, projection, preferred_element_type=jnp.float32)  1.45 us
  transfers between devices with their start and end apart: 2, of which 2 were waited for; matrix products, arithmetic and copies ran while one was open for 1% of the time, Pallas kernels for 0%

commit v1 on v0

v1 whole, which is shorter than its diff:
```python
import jax
import jax.numpy as jnp
from jax import lax
from jax.experimental import pallas as pl
from jax.experimental.pallas import tpu as pltpu
from jax.sharding import PartitionSpec as P

HD = 128
CORES = 2
CHUNKS = 5
EPSILON = 1e-06
ROPE_BASE = 1000000.0
MESH = pl.DeviceIdType.MESH


def inverse_rms(values):
    return lax.rsqrt(jnp.mean(values * values, axis=-1, keepdims=True) + EPSILON)


def tick_kernel(
    sections,
    tensors,
    state_hbm,
    gain_hbm,
    wq_hbm,
    wk_hbm,
    wv_hbm,
    wo_hbm,
    qgain_hbm,
    kgain_hbm,
    ck_hbm,
    cv_hbm,
    len_hbm,
    handed,
    nk_out,
    nv_out,
    state_v,
    gain_v,
    w_v,
    wo_v,
    qgain_v,
    kgain_v,
    ck_v,
    cv_v,
    len_v,
    partial_v,
    arrived_v,
    result_v,
    small_sem,
    w_sem,
    wo_sem,
    part_send,
    part_recv,
    res_send,
    res_recv,
):
    rows, width = state_v.shape
    heads = wq_hbm.shape[2] // HD
    depth = width // CHUNKS
    block = width // tensors
    slots = ck_v.shape[1]

    sec = lax.axis_index("section")
    ten = lax.axis_index("tensor")
    chip, core = ten // CORES, ten % CORES
    chips = tensors // CORES
    after = (sec + 1) % sections
    before = (sec + sections - 1) % sections

    offsets = [(dy, dc) for dy in range(1, chips) for dc in range(CORES)]
    offsets += [(0, dc) for dc in range(1, CORES)] + [(0, 0)]

    def member(offset):
        return ((chip + offset[0]) % chips) * CORES + (core + offset[1]) % CORES

    def origin(offset):
        return ((chip + chips - offset[0]) % chips) * CORES + (
            core + CORES - offset[1]
        ) % CORES

    def columns(which):
        return pl.ds(pl.multiple_of(which * block, 128), block)

    small = [
        pltpu.make_async_copy(source, target, small_sem.at[at])
        for at, (source, target) in enumerate(
            [
                (state_hbm.at[0], state_v),
                (gain_hbm, gain_v),
                (len_hbm, len_v),
                (qgain_hbm, qgain_v),
                (kgain_hbm, kgain_v),
                (ck_hbm.at[0, :, 0], ck_v),
                (cv_hbm.at[0, :, 0], cv_v),
            ]
        )
    ]
    for copy in small[:5]:
        copy.start()
    weights = []
    query_width = heads * HD
    for c in range(CHUNKS):
        span = pl.ds(c * depth, depth)
        weights.append(
            [
                pltpu.make_async_copy(
                    wq_hbm.at[0, span], w_v.at[span, pl.ds(0, query_width)], w_sem.at[c, 0]
                ),
                pltpu.make_async_copy(
                    wk_hbm.at[0, span], w_v.at[span, pl.ds(query_width, HD)], w_sem.at[c, 1]
                ),
                pltpu.make_async_copy(
                    wv_hbm.at[0, span], w_v.at[span, pl.ds(query_width + HD, HD)], w_sem.at[c, 2]
                ),
            ]
        )
        for copy in weights[-1]:
            copy.start()
    for copy in small[5:]:
        copy.start()
    projections = [
        pltpu.make_async_copy(
            wo_hbm.at[0, :, columns(member(offset))], wo_v.at[at], wo_sem.at[at]
        )
        for at, offset in enumerate(offsets)
    ]
    for copy in projections:
        copy.start()

    barrier = pltpu.get_barrier_semaphore()
    for offset in offsets[:-1]:
        pl.semaphore_signal(
            barrier, inc=1, device_id=(sec, member(offset)), device_id_type=MESH
        )
    for offset in offsets:
        pl.semaphore_signal(
            barrier, inc=1, device_id=(before, member(offset)), device_id_type=MESH
        )

    for copy in small[:5]:
        copy.wait()
    hidden = state_v[...].astype(jnp.float32)
    normed = (hidden * inverse_rms(hidden) * gain_v[...].astype(jnp.float32)).astype(jnp.bfloat16)

    on_diagonal = lax.broadcasted_iota(jnp.int32, (rows, rows), 0) == lax.broadcasted_iota(
        jnp.int32, (rows, rows), 1
    )
    spread = jnp.broadcast_to(len_v[...].astype(jnp.float32), (rows, rows))
    position = jnp.sum(jnp.where(on_diagonal, spread, 0.0), axis=1, keepdims=True)
    lane = lax.broadcasted_iota(jnp.int32, (rows, HD), 1)
    half = HD // 2
    index = jnp.where(lane < half, lane, lane - half).astype(jnp.float32)
    frequency = jnp.exp(index * (-2.0 / HD * 13.815510557964274))
    angles = position * frequency
    cosine = jnp.cos(angles)
    sine = jnp.sin(angles)
    sine = jnp.where(lane < half, -sine, sine)

    def rotate(values, cosines, sines):
        return values * cosines + pltpu.roll(values, half, 1) * sines

    gap = (
        lax.broadcasted_iota(jnp.int32, (rows, rows * slots), 1)
        - lax.broadcasted_iota(jnp.int32, (rows, rows * slots), 0) * slots
    ).astype(jnp.float32)
    excluded = jnp.where((gap >= 0.0) & (gap < position), 0.0, -1e30)

    def stacked(values):
        return jnp.concatenate([values] * heads, axis=0)

    cosine_all, sine_all, excluded_all = stacked(cosine), stacked(sine), stacked(excluded)
    query_gain = qgain_v[...].astype(jnp.float32)
    key_gain = kgain_v[...].astype(jnp.float32)

    total = None
    for c in range(CHUNKS):
        for copy in weights[c]:
            copy.wait()
        term = jnp.dot(
            normed[:, c * depth : (c + 1) * depth],
            w_v[c * depth : (c + 1) * depth, :],
            preferred_element_type=jnp.float32,
        )
        total = term if total is None else total + term

    key_raw = total[:, query_width : query_width + HD]
    new_value = total[:, query_width + HD :].astype(jnp.bfloat16)
    new_key = rotate(key_raw * inverse_rms(key_raw) * key_gain, cosine, sine).astype(jnp.bfloat16)
    nk_out[...] = new_key
    nv_out[...] = new_value

    query = jnp.concatenate([total[:, h * HD : (h + 1) * HD] for h in range(heads)], axis=0)
    query_rot = rotate(query * inverse_rms(query) * query_gain, cosine_all, sine_all).astype(
        jnp.bfloat16
    )

    scale = HD**-0.5
    own_score = (
        jnp.sum(
            query_rot.astype(jnp.float32) * stacked(new_key.astype(jnp.float32)),
            axis=1,
            keepdims=True,
        )
        * scale
    )
    small[5].wait()
    keys = ck_v[...].reshape(rows * slots, HD)
    scores = (
        lax.dot_general(
            query_rot, keys, (((1,), (1,)), ((), ())), preferred_element_type=jnp.float32
        )
        * scale
        + excluded_all
    )
    row_max = jnp.maximum(jnp.max(scores, axis=1, keepdims=True), own_score)
    cache_exp = jnp.exp(scores - row_max)
    own_exp = jnp.exp(own_score - row_max)
    share = 1.0 / (jnp.sum(cache_exp, axis=1, keepdims=True) + own_exp)
    cache_prob = (cache_exp * share).astype(jnp.bfloat16)
    own_prob = (own_exp * share).astype(jnp.bfloat16).astype(jnp.float32)
    small[6].wait()
    attended = jnp.dot(
        cache_prob, cv_v[...].reshape(rows * slots, HD), preferred_element_type=jnp.float32
    )
    attended = (attended + own_prob * stacked(new_value.astype(jnp.float32))).astype(jnp.bfloat16)
    attended = jnp.concatenate(
        [attended[h * rows : (h + 1) * rows] for h in range(heads)], axis=1
    )

    pl.semaphore_wait(barrier, 2 * tensors - 1)

    sends = []
    for at, offset in enumerate(offsets):
        projections[at].wait()
        partial = jnp.dot(attended, wo_v[at], preferred_element_type=jnp.float32)
        if at == tensors - 1:
            own = partial
            break
        partial_v[at] = partial
        send = pltpu.make_async_remote_copy(
            src_ref=partial_v.at[at],
            dst_ref=arrived_v.at[at],
            send_sem=part_send.at[at],
            recv_sem=part_recv.at[at],
            device_id=(sec, member(offset)),
            device_id_type=MESH,
        )
        send.start()
        sends.append(send)

    own = own + state_v[:, columns(ten)].astype(jnp.float32)
    for at in reversed(range(tensors - 1)):
        sends[at].wait_recv()
        own = own + arrived_v[at]
    result_v[...] = own.astype(jnp.bfloat16)

    def handing(at, offset, which):
        return pltpu.make_async_remote_copy(
            src_ref=result_v,
            dst_ref=handed.at[:, columns(which)],
            send_sem=res_send.at[at],
            recv_sem=res_recv.at[at],
            device_id=(after, member(offset)),
            device_id_type=MESH,
        )

    for at, offset in enumerate(offsets):
        handing(at, offset, ten).start()
    for send in sends:
        send.wait_send()
    for at, offset in enumerate(offsets):
        handing(at, offset, origin(offset)).wait_recv()
    for at, offset in enumerate(offsets):
        handing(at, offset, ten).wait_send()


def solution(mesh):
    sections, tensors = mesh.shape["section"], mesh.shape["tensor"]

    def body(state, gain_in, w_query, w_key, w_value, w_output, query_gain, key_gain, ck, cv, lengths):
        _, rows, width = state.shape
        query_width = w_query.shape[2]
        slots = ck.shape[3]
        block = width // tensors
        any_spec = pl.BlockSpec(memory_space=pltpu.HBM)
        vmem = pl.BlockSpec(memory_space=pltpu.VMEM)

        def kernel(*refs):
            tick_kernel(sections, tensors, *refs)

        handed, new_key, new_value = pl.pallas_call(
            kernel,
            out_shape=(
                jax.ShapeDtypeStruct((rows, width), jnp.bfloat16),
                jax.ShapeDtypeStruct((rows, HD), jnp.bfloat16),
                jax.ShapeDtypeStruct((rows, HD), jnp.bfloat16),
            ),
            in_specs=[any_spec] * 11,
            out_specs=(vmem, vmem, vmem),
            scratch_shapes=[
                pltpu.VMEM((rows, width), jnp.bfloat16),
                pltpu.VMEM((1, width), jnp.bfloat16),
                pltpu.VMEM((width, query_width + 2 * HD), jnp.bfloat16),
                pltpu.VMEM((tensors, query_width, block), jnp.bfloat16),
                pltpu.VMEM((1, HD), jnp.bfloat16),
                pltpu.VMEM((1, HD), jnp.bfloat16),
                pltpu.VMEM((rows, slots, HD), jnp.bfloat16),
                pltpu.VMEM((rows, slots, HD), jnp.bfloat16),
                pltpu.VMEM((1, rows), jnp.int32),
                pltpu.VMEM((tensors - 1, rows, block), jnp.float32),
                pltpu.VMEM((tensors - 1, rows, block), jnp.float32),
                pltpu.VMEM((rows, block), jnp.bfloat16),
                pltpu.SemaphoreType.DMA((7,)),
                pltpu.SemaphoreType.DMA((CHUNKS, 3)),
                pltpu.SemaphoreType.DMA((tensors,)),
                pltpu.SemaphoreType.DMA((tensors - 1,)),
                pltpu.SemaphoreType.DMA((tensors - 1,)),
                pltpu.SemaphoreType.DMA((tensors,)),
                pltpu.SemaphoreType.DMA((tensors,)),
            ],
            compiler_params=pltpu.CompilerParams(
                collective_id=0, has_side_effects=True, vmem_limit_bytes=63 * 1024 * 1024
            ),
            cost_estimate=pl.CostEstimate(
                flops=4 * rows * width * (query_width + HD),
                bytes_accessed=4 * width * (query_width + HD),
                transcendentals=rows * rows * slots * 8,
            ),
            name="tick",
        )(state, gain_in, w_query, w_key, w_value, w_output, query_gain, key_gain, ck, cv, lengths)
        return (
            handed[None],
            new_key.reshape(1, rows, 1, HD),
            new_value.reshape(1, rows, 1, HD),
        )

    placed = (
        P("section", None, None),
        P("section", None),
        P("section", None, "tensor"),
        P("section", None, "tensor"),
        P("section", None, "tensor"),
        P("section", "tensor", None),
        P("section", None),
        P("section", None),
        P("section", None, "tensor", None, None),
        P("section", None, "tensor", None, None),
        P("section", None),
    )
    return jax.shard_map(
        body,
        mesh=mesh,
        in_specs=placed,
        out_specs=(
            P("section", None, None),
            P("section", None, "tensor", None),
            P("section", None, "tensor", None),
        ),
        check_vma=False,
    )
```

time: 72.5 us -> 23.6 us (0.33)
  waiting for transfers between devices: 39.5 us -> 0 us
  Pallas kernels: 0 us -> 18.7 us
  between operations: 14.2 us -> 0.64 us
  matrix products: 8.84 us -> 0 us
  other arithmetic: 7.52 us -> 0 us
  local copies, waits for them, and re-layouts: 0.68 us -> 4.08 us
  starting transfers between devices: 1.56 us -> 0 us
    psum x1 -> x0, waiting for transfers between devices: 34.4 us -> none  [body(): summed = lax.psum(partial_value, 'tensor')]
    pallas_call x0 -> x1, Pallas kernels: none -> 18.7 us  [body(): pl.pallas_call(kernel, out_shape=(jax.ShapeDtypeStruct((rows, width), jnp...]
    dot_general x7 -> x0, matrix products: 8.84 us -> none  [the longest x1 3.39 us: attend(): jnp.dot(normed, w_query, preferred_element_type=jnp.float32)]
    ppermute x1 -> x0, waiting for transfers between devices: 5 us -> none  [shifted(): return lax.ppermute(value, axis, pairs)]
    convert_element_type x4 -> x0, other arithmetic: 3.47 us -> none  [the longest x2 1.73 us: rms_norm(): gain_vec.astype(jnp.float32)]
    unnamed x12 -> x3, local copies, waits for them, and re-layouts: 0.68 us -> 4.08 us
    ppermute x1 -> x0, starting transfers between devices: 1.52 us -> none  [shifted(): return lax.ppermute(value, axis, pairs)]
    reduce_sum x3 -> x0, other arithmetic: 1.29 us -> none  [the longest x2 1.11 us: rms_norm(): jnp.mean(values * values, axis=-1, keepdims=True) + epsilon]
  transfers between devices with their start and end apart: 2 -> 0, of which waited for: 2 -> 0; matrix products, arithmetic and copies ran while one was open for 1% -> 0% of each run, Pallas kernels for 0% -> 0%
where the time goes in v1:
time: 23.6 us; the launch traced here: 23.4 us
  Pallas kernels  18.7 us (79%)
  local copies, waits for them, and re-layouts  4.08 us (17%)
  between operations  0.64 us (3%)
    pallas_call x1, Pallas kernels, body(): pl.pallas_call(kernel, out_shape=(jax.ShapeDtypeStruct((rows, width), jnp...  18.7 us
    unnamed x3, local copies, waits for them, and re-layouts  4.08 us

profile of v1, /device:TPU:0, one launch (start us, length us, event | category | flops | bytes accessed | tf_op | source)
XLA Modules:
  0.0 23.4 jit_solution(9245058690328481317)
XLA Ops:
  0.6 18.7 %tick.1 = (bf16[16,2560]{1,0:T(8,128)(2,1)}, bf16[16,128]{1,0:T(8,128)(2,1)}, bf16[16,128]{1,0:T(8,128)(2,1)}) custom-call(bf16[1,16,2560]{2,1,0:T(8,128)(2,1)} %refs_0_.1, bf16[1,2560]{1,0:T(2,128)(2,1)} %refs_1_.1, bf16[1,2560,1024]{2,1,0:T(8,128)(2,1)} %refs_2_.1, bf16[1,2560,128]{2,1,0:T(8,128)(2,1)} %refs_3_.1, bf16[1,2560,128]{2,1,0:T(8,128)(2,1)} %refs_4_.1, ...), custom_call_target="tpu_custom_call" | custom-call | flops 188743680 | bytes 11796480 | tf_op jit(solution)/shard_map/tick/pallas_call | solution.py:291
  19.3 1.5 %copy.17 = bf16[1,16,2560]{2,1,0:T(8,128)(2,1)} copy(bf16[1,16,2560]{2,1,0:T(8,128)(2,1)} %bitcast.3) | data formatting | bytes 163840
  20.9 1.3 %copy.18 = bf16[1,16,1,128]{3,1,2,0:T(8,128)(2,1)} copy(bf16[1,16,1,128]{3,1,2,0:T(8,128)(2,1)} %bitcast.5) | data formatting | bytes 8192
  22.1 1.3 %copy.19 = bf16[1,16,1,128]{3,1,2,0:T(8,128)(2,1)} copy(bf16[1,16,1,128]{3,1,2,0:T(8,128)(2,1)} %bitcast.4) | data formatting | bytes 8192

commit v2 on v1

--- a/solution.py
+++ b/solution.py
@@ -274,6 +274,17 @@
         handing(at, offset, ten).wait_send()
 
 
+def store_kernel(*refs):
+    count = (len(refs) - 1) // 2
+    copies = [
+        pltpu.make_async_copy(refs[at], refs[count + at], refs[-1].at[at]) for at in range(count)
+    ]
+    for copy in copies:
+        copy.start()
+    for copy in copies:
+        copy.wait()
+
+
 def solution(mesh):
     sections, tensors = mesh.shape["section"], mesh.shape["tensor"]
 
@@ -282,20 +293,21 @@
         query_width = w_query.shape[2]
         slots = ck.shape[3]
         block = width // tensors
-        any_spec = pl.BlockSpec(memory_space=pltpu.HBM)
+        hbm = pl.BlockSpec(memory_space=pltpu.HBM)
         vmem = pl.BlockSpec(memory_space=pltpu.VMEM)
 
         def kernel(*refs):
             tick_kernel(sections, tensors, *refs)
 
-        handed, new_key, new_value = pl.pallas_call(
+        operands = (
+            state, gain_in, w_query, w_key, w_value, w_output, query_gain, key_gain, ck, cv, lengths
+        )
+        operands = [pltpu.with_memory_space_constraint(x, pltpu.HBM) for x in operands]
+        shapes = ((rows, width), (rows, HD), (rows, HD))
+        results = pl.pallas_call(
             kernel,
-            out_shape=(
-                jax.ShapeDtypeStruct((rows, width), jnp.bfloat16),
-                jax.ShapeDtypeStruct((rows, HD), jnp.bfloat16),
-                jax.ShapeDtypeStruct((rows, HD), jnp.bfloat16),
-            ),
-            in_specs=[any_spec] * 11,
+            out_shape=tuple(pltpu.VMEM(shape, jnp.bfloat16) for shape in shapes),
+            in_specs=[hbm] * 11,
             out_specs=(vmem, vmem, vmem),
             scratch_shapes=[
                 pltpu.VMEM((rows, width), jnp.bfloat16),
@@ -319,7 +331,7 @@
                 pltpu.SemaphoreType.DMA((tensors,)),
             ],
             compiler_params=pltpu.CompilerParams(
-                collective_id=0, has_side_effects=True, vmem_limit_bytes=63 * 1024 * 1024
+                collective_id=0, has_side_effects=True, vmem_limit_bytes=48 * 1024 * 1024
             ),
             cost_estimate=pl.CostEstimate(
                 flops=4 * rows * width * (query_width + HD),
@@ -327,7 +339,16 @@
                 transcendentals=rows * rows * slots * 8,
             ),
             name="tick",
-        )(state, gain_in, w_query, w_key, w_value, w_output, query_gain, key_gain, ck, cv, lengths)
+        )(*operands)
+        handed, new_key, new_value = pl.pallas_call(
+            store_kernel,
+            out_shape=tuple(pltpu.HBM(shape, jnp.bfloat16) for shape in shapes),
+            in_specs=[vmem] * 3,
+            out_specs=(hbm, hbm, hbm),
+            scratch_shapes=[pltpu.SemaphoreType.DMA((3,))],
+            compiler_params=pltpu.CompilerParams(vmem_limit_bytes=8 * 1024 * 1024),
+            name="store",
+        )(*results)
         return (
             handed[None],
             new_key.reshape(1, rows, 1, HD),

time: 23.6 us -> 19.5 us (0.83)
  local copies, waits for them, and re-layouts: 4.08 us -> 0 us
    unnamed x3 -> x0, local copies, waits for them, and re-layouts: 4.08 us -> none
    pallas_call x1 -> x2, Pallas kernels: 18.7 us -> 18.7 us  [the longest x1 18.1 us: body(): pl.pallas_call(kernel, out_shape=tuple((pltpu.VMEM(shape, jnp.bfloat16) f...]
where the time goes in v2:
time: 19.5 us; the launch traced here: 19.4 us
  Pallas kernels  18.7 us (96%)
  between operations  0.64 us (3%)
    pallas_call x1, Pallas kernels, body(): pl.pallas_call(kernel, out_shape=tuple((pltpu.VMEM(shape, jnp.bfloat16) f...  18.1 us
    pallas_call x1, Pallas kernels, body(): pl.pallas_call(store_kernel, out_shape=tuple((pltpu.HBM(shape, jnp.bfloat...  0.67 us

profile of v2, /device:TPU:0, one launch (start us, length us, event | category | flops | bytes accessed | tf_op | source)
XLA Modules:
  0.0 19.4 jit_solution(6813326425473163504)
XLA Ops:
  0.6 18.1 %tick.1 = (bf16[16,2560]{1,0:T(8,128)(2,1)S(1)}, bf16[16,128]{1,0:T(8,128)(2,1)S(1)}, bf16[16,128]{1,0:T(8,128)(2,1)S(1)}) custom-call(bf16[1,16,2560]{2,1,0:T(8,128)(2,1)} %refs_0_.1, bf16[1,2560]{1,0:T(2,128)(2,1)} %refs_1_.1, bf16[1,2560,1024]{2,1,0:T(8,128)(2,1)} %refs_2_.1, bf16[1,2560,128]{2,1,0:T(8,128)(2,1)} %refs_3_.1, ...), custom_call_target="tpu_custom_call" | custom-call | flops 188743680 | bytes 11796480 | tf_op jit(solution)/shard_map/tick/pallas_call | solution.py:307
  18.7 0.7 %store.1 = (bf16[16,2560]{1,0:T(8,128)(2,1)}, bf16[16,128]{1,0:T(8,128)(2,1)}, bf16[16,128]{1,0:T(8,128)(2,1)}) custom-call(bf16[16,2560]{1,0:T(8,128)(2,1)S(1)} %get-tuple-element.9.refs_0_, bf16[16,128]{1,0:T(8,128)(2,1)S(1)} %get-tuple-element.10.refs_1_, bf16[16,128]{1,0:T(8,128)(2,1)S(1)} %get-tuple-element.11.refs_2_), custom_call_target="tpu_custom_call" | custom-call | tf_op jit(solution)/shard_map/store/pallas_call | solution.py:343

commit v3 on v2

--- a/solution.py
+++ b/solution.py
@@ -15,6 +15,11 @@
 
 def inverse_rms(values):
     return lax.rsqrt(jnp.mean(values * values, axis=-1, keepdims=True) + EPSILON)
+
+
+def part_starts(block):
+    first = block // 128 * 2 // 5 * 128
+    return ((0, first), (first, block - first))
 
 
 def tick_kernel(
@@ -43,8 +48,10 @@
     ck_v,
     cv_v,
     len_v,
-    partial_v,
-    arrived_v,
+    far_v,
+    far_arrived_v,
+    near_v,
+    near_arrived_v,
     result_v,
     small_sem,
     w_sem,
@@ -229,49 +236,66 @@
 
     pl.semaphore_wait(barrier, 2 * tensors - 1)
 
-    sends = []
-    for at, offset in enumerate(offsets):
-        projections[at].wait()
-        partial = jnp.dot(attended, wo_v[at], preferred_element_type=jnp.float32)
-        if at == tensors - 1:
-            own = partial
-            break
-        partial_v[at] = partial
-        send = pltpu.make_async_remote_copy(
-            src_ref=partial_v.at[at],
-            dst_ref=arrived_v.at[at],
-            send_sem=part_send.at[at],
-            recv_sem=part_recv.at[at],
-            device_id=(sec, member(offset)),
-            device_id_type=MESH,
-        )
-        send.start()
-        sends.append(send)
-
-    own = own + state_v[:, columns(ten)].astype(jnp.float32)
-    for at in reversed(range(tensors - 1)):
-        sends[at].wait_recv()
-        own = own + arrived_v[at]
-    result_v[...] = own.astype(jnp.bfloat16)
-
-    def handing(at, offset, which):
+    far = tensors - CORES
+    starts = part_starts(block)
+    sends, own = [], []
+    for part, (start, size) in enumerate(starts):
+        sends.append([])
+        for at, offset in enumerate(offsets):
+            if part == 0:
+                projections[at].wait()
+            partial = jnp.dot(
+                attended, wo_v[at, :, start : start + size], preferred_element_type=jnp.float32
+            )
+            if at == tensors - 1:
+                own.append(partial)
+                break
+            if at < far:
+                source, target = far_v[part].at[at], far_arrived_v[part].at[at]
+            else:
+                source, target = near_v[part].at[at - far], near_arrived_v[part].at[at - far]
+            source[...] = partial.astype(source.dtype)
+            send = pltpu.make_async_remote_copy(
+                src_ref=source,
+                dst_ref=target,
+                send_sem=part_send.at[part, at],
+                recv_sem=part_recv.at[part, at],
+                device_id=(sec, member(offset)),
+                device_id_type=MESH,
+            )
+            send.start()
+            sends[-1].append((send, target))
+
+    def handing(part, at, offset, which):
+        start, size = starts[part]
+        span = pl.ds(pl.multiple_of(which * block + start, 128), size)
         return pltpu.make_async_remote_copy(
-            src_ref=result_v,
-            dst_ref=handed.at[:, columns(which)],
-            send_sem=res_send.at[at],
-            recv_sem=res_recv.at[at],
+            src_ref=result_v[part],
+            dst_ref=handed.at[:, span],
+            send_sem=res_send.at[part, at],
+            recv_sem=res_recv.at[part, at],
             device_id=(after, member(offset)),
             device_id_type=MESH,
         )
 
-    for at, offset in enumerate(offsets):
-        handing(at, offset, ten).start()
-    for send in sends:
-        send.wait_send()
-    for at, offset in enumerate(offsets):
-        handing(at, offset, origin(offset)).wait_recv()
-    for at, offset in enumerate(offsets):
-        handing(at, offset, ten).wait_send()
+    for part, (start, size) in enumerate(starts):
+        span = pl.ds(pl.multiple_of(ten * block + start, 128), size)
+        result = own[part] + state_v[:, span].astype(jnp.float32)
+        for send, target in reversed(sends[part]):
+            send.wait_recv()
+            result = result + target[...].astype(jnp.float32)
+        result_v[part][...] = result.astype(jnp.bfloat16)
+        for at, offset in enumerate(offsets):
+            handing(part, at, offset, ten).start()
+    for part in range(len(starts)):
+        for send, _ in sends[part]:
+            send.wait_send()
+    for part in range(len(starts)):
+        for at, offset in enumerate(offsets):
+            handing(part, at, offset, origin(offset)).wait_recv()
+    for part in range(len(starts)):
+        for at, offset in enumerate(offsets):
+            handing(part, at, offset, ten).wait_send()
 
 
 def store_kernel(*refs):
@@ -293,6 +317,8 @@
         query_width = w_query.shape[2]
         slots = ck.shape[3]
         block = width // tensors
+        far = tensors - CORES
+        sizes = [size for _, size in part_starts(block)]
         hbm = pl.BlockSpec(memory_space=pltpu.HBM)
         vmem = pl.BlockSpec(memory_space=pltpu.VMEM)
 
@@ -319,16 +345,18 @@
                 pltpu.VMEM((rows, slots, HD), jnp.bfloat16),
                 pltpu.VMEM((rows, slots, HD), jnp.bfloat16),
                 pltpu.VMEM((1, rows), jnp.int32),
-                pltpu.VMEM((tensors - 1, rows, block), jnp.float32),
-                pltpu.VMEM((tensors - 1, rows, block), jnp.float32),
-                pltpu.VMEM((rows, block), jnp.bfloat16),
+                [pltpu.VMEM((far, rows, size), jnp.bfloat16) for size in sizes],
+                [pltpu.VMEM((far, rows, size), jnp.bfloat16) for size in sizes],
+                [pltpu.VMEM((CORES - 1, rows, size), jnp.float32) for size in sizes],
+                [pltpu.VMEM((CORES - 1, rows, size), jnp.float32) for size in sizes],
+                [pltpu.VMEM((rows, size), jnp.bfloat16) for size in sizes],
                 pltpu.SemaphoreType.DMA((7,)),
                 pltpu.SemaphoreType.DMA((CHUNKS, 3)),
                 pltpu.SemaphoreType.DMA((tensors,)),
-                pltpu.SemaphoreType.DMA((tensors - 1,)),
-                pltpu.SemaphoreType.DMA((tensors - 1,)),
-                pltpu.SemaphoreType.DMA((tensors,)),
-                pltpu.SemaphoreType.DMA((tensors,)),
+                pltpu.SemaphoreType.DMA((len(sizes), tensors - 1)),
+                pltpu.SemaphoreType.DMA((len(sizes), tensors - 1)),
+                pltpu.SemaphoreType.DMA((len(sizes), tensors)),
+                pltpu.SemaphoreType.DMA((len(sizes), tensors)),
             ],
             compiler_params=pltpu.CompilerParams(
                 collective_id=0, has_side_effects=True, vmem_limit_bytes=48 * 1024 * 1024

time: 19.5 us -> 19.3 us (0.990)
  no operation moved by 1% of the time
where the time goes in v3:
time: 19.3 us; the launch traced here: 19.2 us
  Pallas kernels  18.6 us (96%)
  between operations  0.64 us (3%)
    pallas_call x1, Pallas kernels, body(): pl.pallas_call(kernel, out_shape=tuple((pltpu.VMEM(shape, jnp.bfloat16) f...  17.9 us
    pallas_call x1, Pallas kernels, body(): pl.pallas_call(store_kernel, out_shape=tuple((pltpu.HBM(shape, jnp.bfloat...  0.67 us

profile of v3, /device:TPU:0, one launch (start us, length us, event | category | flops | bytes accessed | tf_op | source)
XLA Modules:
  0.0 19.2 jit_solution(14949530777454177999)
XLA Ops:
  0.6 17.9 %tick.1 = (bf16[16,2560]{1,0:T(8,128)(2,1)S(1)}, bf16[16,128]{1,0:T(8,128)(2,1)S(1)}, bf16[16,128]{1,0:T(8,128)(2,1)S(1)}) custom-call(bf16[1,16,2560]{2,1,0:T(8,128)(2,1)} %refs_0_.1, bf16[1,2560]{1,0:T(2,128)(2,1)} %refs_1_.1, bf16[1,2560,1024]{2,1,0:T(8,128)(2,1)} %refs_2_.1, bf16[1,2560,128]{2,1,0:T(8,128)(2,1)} %refs_3_.1, ...), custom_call_target="tpu_custom_call" | custom-call | flops 188743680 | bytes 11796480 | tf_op jit(solution)/shard_map/tick/pallas_call | solution.py:333
  18.5 0.7 %store.1 = (bf16[16,2560]{1,0:T(8,128)(2,1)}, bf16[16,128]{1,0:T(8,128)(2,1)}, bf16[16,128]{1,0:T(8,128)(2,1)}) custom-call(bf16[16,2560]{1,0:T(8,128)(2,1)S(1)} %get-tuple-element.9.refs_0_, bf16[16,128]{1,0:T(8,128)(2,1)S(1)} %get-tuple-element.10.refs_1_, bf16[16,128]{1,0:T(8,128)(2,1)S(1)} %get-tuple-element.11.refs_2_), custom_call_target="tpu_custom_call" | custom-call | tf_op jit(solution)/shard_map/store/pallas_call | solution.py:371

commit v4 on v2

--- a/solution.py
+++ b/solution.py
@@ -7,7 +7,7 @@
 
 HD = 128
 CORES = 2
-CHUNKS = 5
+GROUPS = 2
 EPSILON = 1e-06
 ROPE_BASE = 1000000.0
 MESH = pl.DeviceIdType.MESH
@@ -36,18 +36,20 @@
     nv_out,
     state_v,
     gain_v,
-    w_v,
+    wkv_v,
+    wq_v,
     wo_v,
     qgain_v,
     kgain_v,
     ck_v,
     cv_v,
     len_v,
-    partial_v,
+    total_v,
     arrived_v,
     result_v,
     small_sem,
-    w_sem,
+    wkv_sem,
+    wq_sem,
     wo_sem,
     part_send,
     part_recv,
@@ -56,7 +58,8 @@
 ):
     rows, width = state_v.shape
     heads = wq_hbm.shape[2] // HD
-    depth = width // CHUNKS
+    members = heads // GROUPS
+    span = members * HD
     block = width // tensors
     slots = ck_v.shape[1]
 
@@ -97,35 +100,24 @@
     ]
     for copy in small[:5]:
         copy.start()
-    weights = []
-    query_width = heads * HD
-    for c in range(CHUNKS):
-        span = pl.ds(c * depth, depth)
-        weights.append(
-            [
-                pltpu.make_async_copy(
-                    wq_hbm.at[0, span], w_v.at[span, pl.ds(0, query_width)], w_sem.at[c, 0]
-                ),
-                pltpu.make_async_copy(
-                    wk_hbm.at[0, span], w_v.at[span, pl.ds(query_width, HD)], w_sem.at[c, 1]
-                ),
-                pltpu.make_async_copy(
-                    wv_hbm.at[0, span], w_v.at[span, pl.ds(query_width + HD, HD)], w_sem.at[c, 2]
-                ),
-            ]
-        )
-        for copy in weights[-1]:
-            copy.start()
-    for copy in small[5:]:
+    pair = [
+        pltpu.make_async_copy(source.at[0], wkv_v.at[:, pl.ds(at * HD, HD)], wkv_sem.at[at])
+        for at, source in enumerate((wk_hbm, wv_hbm))
+    ]
+    queries = [
+        pltpu.make_async_copy(wq_hbm.at[0, :, pl.ds(g * span, span)], wq_v.at[g], wq_sem.at[g])
+        for g in range(GROUPS)
+    ]
+    projections = [
+        pltpu.make_async_copy(wo_hbm.at[0, pl.ds(g * span, span)], wo_v.at[g], wo_sem.at[g])
+        for g in range(GROUPS)
+    ]
+    for copy in pair + queries[:1] + small[5:]:
         copy.start()
-    projections = [
-        pltpu.make_async_copy(
-            wo_hbm.at[0, :, columns(member(offset))], wo_v.at[at], wo_sem.at[at]
-        )
-        for at, offset in enumerate(offsets)
-    ]
-    for copy in projections:
-        copy.start()
+    for g in range(GROUPS):
+        if g + 1 < GROUPS:
+            queries[g + 1].start()
+        projections[g].start()
 
     barrier = pltpu.get_barrier_semaphore()
     for offset in offsets[:-1]:
@@ -166,79 +158,82 @@
     excluded = jnp.where((gap >= 0.0) & (gap < position), 0.0, -1e30)
 
     def stacked(values):
-        return jnp.concatenate([values] * heads, axis=0)
+        return jnp.concatenate([values] * members, axis=0)
 
     cosine_all, sine_all, excluded_all = stacked(cosine), stacked(sine), stacked(excluded)
     query_gain = qgain_v[...].astype(jnp.float32)
     key_gain = kgain_v[...].astype(jnp.float32)
 
-    total = None
-    for c in range(CHUNKS):
-        for copy in weights[c]:
-            copy.wait()
-        term = jnp.dot(
-            normed[:, c * depth : (c + 1) * depth],
-            w_v[c * depth : (c + 1) * depth, :],
-            preferred_element_type=jnp.float32,
-        )
-        total = term if total is None else total + term
-
-    key_raw = total[:, query_width : query_width + HD]
-    new_value = total[:, query_width + HD :].astype(jnp.bfloat16)
+    def project(g):
+        queries[g].wait()
+        return jnp.dot(normed, wq_v[g], preferred_element_type=jnp.float32)
+
+    for copy in pair:
+        copy.wait()
+    both = jnp.dot(normed, wkv_v[...], preferred_element_type=jnp.float32)
+    query = project(0)
+    key_raw = both[:, :HD]
+    new_value = both[:, HD:].astype(jnp.bfloat16)
     new_key = rotate(key_raw * inverse_rms(key_raw) * key_gain, cosine, sine).astype(jnp.bfloat16)
     nk_out[...] = new_key
     nv_out[...] = new_value
-
-    query = jnp.concatenate([total[:, h * HD : (h + 1) * HD] for h in range(heads)], axis=0)
-    query_rot = rotate(query * inverse_rms(query) * query_gain, cosine_all, sine_all).astype(
-        jnp.bfloat16
-    )
+    own_keys = stacked(new_key.astype(jnp.float32))
+    own_values = stacked(new_value.astype(jnp.float32))
+    for copy in small[5:]:
+        copy.wait()
 
     scale = HD**-0.5
-    own_score = (
-        jnp.sum(
-            query_rot.astype(jnp.float32) * stacked(new_key.astype(jnp.float32)),
-            axis=1,
-            keepdims=True,
-        )
-        * scale
-    )
-    small[5].wait()
-    keys = ck_v[...].reshape(rows * slots, HD)
-    scores = (
-        lax.dot_general(
-            query_rot, keys, (((1,), (1,)), ((), ())), preferred_element_type=jnp.float32
-        )
-        * scale
-        + excluded_all
-    )
-    row_max = jnp.maximum(jnp.max(scores, axis=1, keepdims=True), own_score)
-    cache_exp = jnp.exp(scores - row_max)
-    own_exp = jnp.exp(own_score - row_max)
-    share = 1.0 / (jnp.sum(cache_exp, axis=1, keepdims=True) + own_exp)
-    cache_prob = (cache_exp * share).astype(jnp.bfloat16)
-    own_prob = (own_exp * share).astype(jnp.bfloat16).astype(jnp.float32)
-    small[6].wait()
-    attended = jnp.dot(
-        cache_prob, cv_v[...].reshape(rows * slots, HD), preferred_element_type=jnp.float32
-    )
-    attended = (attended + own_prob * stacked(new_value.astype(jnp.float32))).astype(jnp.bfloat16)
-    attended = jnp.concatenate(
-        [attended[h * rows : (h + 1) * rows] for h in range(heads)], axis=1
-    )
+
+    def attend(query):
+        query = jnp.concatenate([query[:, h * HD : (h + 1) * HD] for h in range(members)], axis=0)
+        query_rot = rotate(query * inverse_rms(query) * query_gain, cosine_all, sine_all).astype(
+            jnp.bfloat16
+        )
+        own_score = (
+            jnp.sum(query_rot.astype(jnp.float32) * own_keys, axis=1, keepdims=True) * scale
+        )
+        scores = (
+            lax.dot_general(
+                query_rot,
+                ck_v[...].reshape(rows * slots, HD),
+                (((1,), (1,)), ((), ())),
+                preferred_element_type=jnp.float32,
+            )
+            * scale
+            + excluded_all
+        )
+        row_max = jnp.maximum(jnp.max(scores, axis=1, keepdims=True), own_score)
+        cache_exp = jnp.exp(scores - row_max)
+        own_exp = jnp.exp(own_score - row_max)
+        share = 1.0 / (jnp.sum(cache_exp, axis=1, keepdims=True) + own_exp)
+        cache_prob = (cache_exp * share).astype(jnp.bfloat16)
+        own_prob = (own_exp * share).astype(jnp.bfloat16).astype(jnp.float32)
+        attended = jnp.dot(
+            cache_prob, cv_v[...].reshape(rows * slots, HD), preferred_element_type=jnp.float32
+        )
+        attended = (attended + own_prob * own_values).astype(jnp.bfloat16)
+        return jnp.concatenate(
+            [attended[h * rows : (h + 1) * rows] for h in range(members)], axis=1
+        )
+
+    attended = None
+    for g in range(GROUPS + 1):
+        if 0 < g:
+            projections[g - 1].wait()
+        later = project(g + 1) if g + 1 < GROUPS else None
+        if 0 < g:
+            term = jnp.dot(attended, wo_v[g - 1], preferred_element_type=jnp.float32)
+            total_v[...] = term if g == 1 else total_v[...] + term
+        if g < GROUPS:
+            attended = attend(query)
+        query = later
 
     pl.semaphore_wait(barrier, 2 * tensors - 1)
 
     sends = []
-    for at, offset in enumerate(offsets):
-        projections[at].wait()
-        partial = jnp.dot(attended, wo_v[at], preferred_element_type=jnp.float32)
-        if at == tensors - 1:
-            own = partial
-            break
-        partial_v[at] = partial
+    for at, offset in enumerate(offsets[:-1]):
         send = pltpu.make_async_remote_copy(
-            src_ref=partial_v.at[at],
+            src_ref=total_v.at[:, columns(member(offset))],
             dst_ref=arrived_v.at[at],
             send_sem=part_send.at[at],
             recv_sem=part_recv.at[at],
@@ -248,7 +243,7 @@
         send.start()
         sends.append(send)
 
-    own = own + state_v[:, columns(ten)].astype(jnp.float32)
+    own = total_v[:, columns(ten)] + state_v[:, columns(ten)].astype(jnp.float32)
     for at in reversed(range(tensors - 1)):
         sends[at].wait_recv()
         own = own + arrived_v[at]
@@ -312,19 +307,21 @@
             scratch_shapes=[
                 pltpu.VMEM((rows, width), jnp.bfloat16),
                 pltpu.VMEM((1, width), jnp.bfloat16),
-                pltpu.VMEM((width, query_width + 2 * HD), jnp.bfloat16),
-                pltpu.VMEM((tensors, query_width, block), jnp.bfloat16),
+                pltpu.VMEM((width, 2 * HD), jnp.bfloat16),
+                pltpu.VMEM((GROUPS, width, query_width // GROUPS), jnp.bfloat16),
+                pltpu.VMEM((GROUPS, query_width // GROUPS, width), jnp.bfloat16),
                 pltpu.VMEM((1, HD), jnp.bfloat16),
                 pltpu.VMEM((1, HD), jnp.bfloat16),
                 pltpu.VMEM((rows, slots, HD), jnp.bfloat16),
                 pltpu.VMEM((rows, slots, HD), jnp.bfloat16),
                 pltpu.VMEM((1, rows), jnp.int32),
-                pltpu.VMEM((tensors - 1, rows, block), jnp.float32),
+                pltpu.VMEM((rows, width), jnp.float32),
                 pltpu.VMEM((tensors - 1, rows, block), jnp.float32),
                 pltpu.VMEM((rows, block), jnp.bfloat16),
                 pltpu.SemaphoreType.DMA((7,)),
-                pltpu.SemaphoreType.DMA((CHUNKS, 3)),
-                pltpu.SemaphoreType.DMA((tensors,)),
+                pltpu.SemaphoreType.DMA((2,)),
+                pltpu.SemaphoreType.DMA((GROUPS,)),
+                pltpu.SemaphoreType.DMA((GROUPS,)),
                 pltpu.SemaphoreType.DMA((tensors - 1,)),
                 pltpu.SemaphoreType.DMA((tensors - 1,)),
                 pltpu.SemaphoreType.DMA((tensors,)),

time: 19.5 us -> 20.3 us (1.041)
  Pallas kernels: 18.7 us -> 19.6 us
    pallas_call x1, Pallas kernels: 18.1 us -> 18.9 us  [body(): pl.pallas_call(kernel, out_shape=tuple((pltpu.VMEM(shape, jnp.bfloat16) f...]
where the time goes in v4:
time: 20.3 us; the launch traced here: 20.2 us
  Pallas kernels  19.6 us (97%)
  between operations  0.64 us (3%)
    pallas_call x1, Pallas kernels, body(): pl.pallas_call(kernel, out_shape=tuple((pltpu.VMEM(shape, jnp.bfloat16) f...  18.9 us
    pallas_call x1, Pallas kernels, body(): pl.pallas_call(store_kernel, out_shape=tuple((pltpu.HBM(shape, jnp.bfloat...  0.67 us

profile of v4, /device:TPU:0, one launch (start us, length us, event | category | flops | bytes accessed | tf_op | source)
XLA Modules:
  0.0 20.2 jit_solution(1077661040008677312)
XLA Ops:
  0.6 18.9 %tick.1 = (bf16[16,2560]{1,0:T(8,128)(2,1)S(1)}, bf16[16,128]{1,0:T(8,128)(2,1)S(1)}, bf16[16,128]{1,0:T(8,128)(2,1)S(1)}) custom-call(bf16[1,16,2560]{2,1,0:T(8,128)(2,1)} %refs_0_.1, bf16[1,2560]{1,0:T(2,128)(2,1)} %refs_1_.1, bf16[1,2560,1024]{2,1,0:T(8,128)(2,1)} %refs_2_.1, bf16[1,2560,128]{2,1,0:T(8,128)(2,1)} %refs_3_.1, ...), custom_call_target="tpu_custom_call" | custom-call | flops 188743680 | bytes 11796480 | tf_op jit(solution)/shard_map/tick/pallas_call | solution.py:302
  19.5 0.7 %store.1 = (bf16[16,2560]{1,0:T(8,128)(2,1)}, bf16[16,128]{1,0:T(8,128)(2,1)}, bf16[16,128]{1,0:T(8,128)(2,1)}) custom-call(bf16[16,2560]{1,0:T(8,128)(2,1)S(1)} %get-tuple-element.9.refs_0_, bf16[16,128]{1,0:T(8,128)(2,1)S(1)} %get-tuple-element.10.refs_1_, bf16[16,128]{1,0:T(8,128)(2,1)S(1)} %get-tuple-element.11.refs_2_), custom_call_target="tpu_custom_call" | custom-call | tf_op jit(solution)/shard_map/store/pallas_call | solution.py:340

commit v5 on v2

--- a/solution.py
+++ b/solution.py
@@ -36,7 +36,9 @@
     nv_out,
     state_v,
     gain_v,
+    normed_v,
     w_v,
+    total_v,
     wo_v,
     qgain_v,
     kgain_v,
@@ -97,35 +99,37 @@
     ]
     for copy in small[:5]:
         copy.start()
-    weights = []
     query_width = heads * HD
+
+    def weights(c):
+        span = pl.ds(pl.multiple_of(c * depth, depth), depth)
+        return [
+            pltpu.make_async_copy(
+                wq_hbm.at[0, span], w_v.at[span, pl.ds(0, query_width)], w_sem.at[c, 0]
+            ),
+            pltpu.make_async_copy(
+                wk_hbm.at[0, span], w_v.at[span, pl.ds(query_width, HD)], w_sem.at[c, 1]
+            ),
+            pltpu.make_async_copy(
+                wv_hbm.at[0, span], w_v.at[span, pl.ds(query_width + HD, HD)], w_sem.at[c, 2]
+            ),
+        ]
+
     for c in range(CHUNKS):
-        span = pl.ds(c * depth, depth)
-        weights.append(
-            [
-                pltpu.make_async_copy(
-                    wq_hbm.at[0, span], w_v.at[span, pl.ds(0, query_width)], w_sem.at[c, 0]
-                ),
-                pltpu.make_async_copy(
-                    wk_hbm.at[0, span], w_v.at[span, pl.ds(query_width, HD)], w_sem.at[c, 1]
-                ),
-                pltpu.make_async_copy(
-                    wv_hbm.at[0, span], w_v.at[span, pl.ds(query_width + HD, HD)], w_sem.at[c, 2]
-                ),
-            ]
-        )
-        for copy in weights[-1]:
+        for copy in weights(c):
             copy.start()
     for copy in small[5:]:
         copy.start()
+
+    chip_order = [(chip + 1 + h) % chips for h in range(chips)]
     projections = [
         pltpu.make_async_copy(
-            wo_hbm.at[0, :, columns(member(offset))], wo_v.at[at], wo_sem.at[at]
-        )
-        for at, offset in enumerate(offsets)
+            wo_hbm.at[0, :, pl.ds(pl.multiple_of(which * CORES * block, 128), CORES * block)],
+            wo_v.at[h],
+            wo_sem.at[h],
+        )
+        for h, which in enumerate(chip_order)
     ]
-    for copy in projections:
-        copy.start()
 
     barrier = pltpu.get_barrier_semaphore()
     for offset in offsets[:-1]:
@@ -141,6 +145,9 @@
         copy.wait()
     hidden = state_v[...].astype(jnp.float32)
     normed = (hidden * inverse_rms(hidden) * gain_v[...].astype(jnp.float32)).astype(jnp.bfloat16)
+    for c in range(CHUNKS):
+        normed_v[c] = normed[:, c * depth : (c + 1) * depth]
+    total_v[...] = jnp.zeros_like(total_v)
 
     on_diagonal = lax.broadcasted_iota(jnp.int32, (rows, rows), 0) == lax.broadcasted_iota(
         jnp.int32, (rows, rows), 1
@@ -172,16 +179,21 @@
     query_gain = qgain_v[...].astype(jnp.float32)
     key_gain = kgain_v[...].astype(jnp.float32)
 
-    total = None
-    for c in range(CHUNKS):
-        for copy in weights[c]:
+    def project(c, carry):
+        for copy in weights(c):
             copy.wait()
-        term = jnp.dot(
-            normed[:, c * depth : (c + 1) * depth],
-            w_v[c * depth : (c + 1) * depth, :],
-            preferred_element_type=jnp.float32,
-        )
-        total = term if total is None else total + term
+
+        @pl.when(c == 1)
+        def _():
+            for copy in projections:
+                copy.start()
+
+        span = pl.ds(pl.multiple_of(c * depth, depth), depth)
+        total_v[...] += jnp.dot(normed_v[c], w_v[span, :], preferred_element_type=jnp.float32)
+        return carry
+
+    lax.fori_loop(0, CHUNKS, project, 0)
+    total = total_v[...]
 
     key_raw = total[:, query_width : query_width + HD]
     new_value = total[:, query_width + HD :].astype(jnp.bfloat16)
@@ -229,29 +241,37 @@
 
     pl.semaphore_wait(barrier, 2 * tensors - 1)
 
+    def sending(h, source, target, which):
+        return pltpu.make_async_remote_copy(
+            src_ref=partial_v.at[h, source],
+            dst_ref=arrived_v.at[h, target],
+            send_sem=part_send.at[h, source],
+            recv_sem=part_recv.at[h, target],
+            device_id=(sec, which),
+            device_id_type=MESH,
+        )
+
     sends = []
-    for at, offset in enumerate(offsets):
-        projections[at].wait()
-        partial = jnp.dot(attended, wo_v[at], preferred_element_type=jnp.float32)
-        if at == tensors - 1:
-            own = partial
-            break
-        partial_v[at] = partial
-        send = pltpu.make_async_remote_copy(
-            src_ref=partial_v.at[at],
-            dst_ref=arrived_v.at[at],
-            send_sem=part_send.at[at],
-            recv_sem=part_recv.at[at],
-            device_id=(sec, member(offset)),
-            device_id_type=MESH,
-        )
-        send.start()
-        sends.append(send)
-
-    own = own + state_v[:, columns(ten)].astype(jnp.float32)
-    for at in reversed(range(tensors - 1)):
-        sends[at].wait_recv()
-        own = own + arrived_v[at]
+    other = (core + 1) % CORES
+    for h, which in enumerate(chip_order):
+        projections[h].wait()
+        partial = jnp.dot(attended, wo_v[h], preferred_element_type=jnp.float32)
+        for c in range(CORES):
+            partial_v[h, c] = partial[:, c * block : (c + 1) * block]
+        if h < chips - 1:
+            sends += [sending(h, c, core, which * CORES + c) for c in range(CORES)]
+        else:
+            sends += [sending(h, other, core, chip * CORES + other)]
+        for send in sends[-CORES if h < chips - 1 else -1 :]:
+            send.start()
+
+    own = partial_v[chips - 1, core] + state_v[:, columns(ten)].astype(jnp.float32)
+    sending(chips - 1, core, other, chip * CORES + other).wait_recv()
+    own = own + arrived_v[chips - 1, other]
+    for h in range(chips - 1):
+        for c in range(CORES):
+            sending(h, c, c, chip_order[h] * CORES + c).wait_recv()
+            own = own + arrived_v[h, c]
     result_v[...] = own.astype(jnp.bfloat16)
 
     def handing(at, offset, which):
@@ -293,6 +313,7 @@
         query_width = w_query.shape[2]
         slots = ck.shape[3]
         block = width // tensors
+        chips = tensors // CORES
         hbm = pl.BlockSpec(memory_space=pltpu.HBM)
         vmem = pl.BlockSpec(memory_space=pltpu.VMEM)
 
@@ -312,21 +333,23 @@
             scratch_shapes=[
                 pltpu.VMEM((rows, width), jnp.bfloat16),
                 pltpu.VMEM((1, width), jnp.bfloat16),
+                pltpu.VMEM((CHUNKS, rows, width // CHUNKS), jnp.bfloat16),
                 pltpu.VMEM((width, query_width + 2 * HD), jnp.bfloat16),
-                pltpu.VMEM((tensors, query_width, block), jnp.bfloat16),
+                pltpu.VMEM((rows, query_width + 2 * HD), jnp.float32),
+                pltpu.VMEM((chips, query_width, CORES * block), jnp.bfloat16),
                 pltpu.VMEM((1, HD), jnp.bfloat16),
                 pltpu.VMEM((1, HD), jnp.bfloat16),
                 pltpu.VMEM((rows, slots, HD), jnp.bfloat16),
                 pltpu.VMEM((rows, slots, HD), jnp.bfloat16),
                 pltpu.VMEM((1, rows), jnp.int32),
-                pltpu.VMEM((tensors - 1, rows, block), jnp.float32),
-                pltpu.VMEM((tensors - 1, rows, block), jnp.float32),
+                pltpu.VMEM((chips, CORES, rows, block), jnp.float32),
+                pltpu.VMEM((chips, CORES, rows, block), jnp.float32),
                 pltpu.VMEM((rows, block), jnp.bfloat16),
                 pltpu.SemaphoreType.DMA((7,)),
                 pltpu.SemaphoreType.DMA((CHUNKS, 3)),
-                pltpu.SemaphoreType.DMA((tensors,)),
-                pltpu.SemaphoreType.DMA((tensors - 1,)),
-                pltpu.SemaphoreType.DMA((tensors - 1,)),
+                pltpu.SemaphoreType.DMA((chips,)),
+                pltpu.SemaphoreType.DMA((chips, CORES)),
+                pltpu.SemaphoreType.DMA((chips, CORES)),
                 pltpu.SemaphoreType.DMA((tensors,)),
                 pltpu.SemaphoreType.DMA((tensors,)),
             ],

time: 19.5 us -> 19.4 us (level)
  no operation moved by 1% of the time
where the time goes in v5:
time: 19.4 us; the launch traced here: 19.3 us
  Pallas kernels  18.6 us (96%)
  between operations  0.64 us (3%)
    pallas_call x1, Pallas kernels, body(): pl.pallas_call(kernel, out_shape=tuple((pltpu.VMEM(shape, jnp.bfloat16) f...  18 us
    pallas_call x1, Pallas kernels, body(): pl.pallas_call(store_kernel, out_shape=tuple((pltpu.HBM(shape, jnp.bfloat...  0.67 us

profile of v5, /device:TPU:0, one launch (start us, length us, event | category | flops | bytes accessed | tf_op | source)
XLA Modules:
  0.0 19.3 jit_solution(786798029859127042)
XLA Ops:
  0.6 18.0 %tick.1 = (bf16[16,2560]{1,0:T(8,128)(2,1)S(1)}, bf16[16,128]{1,0:T(8,128)(2,1)S(1)}, bf16[16,128]{1,0:T(8,128)(2,1)S(1)}) custom-call(bf16[1,16,2560]{2,1,0:T(8,128)(2,1)} %refs_0_.1, bf16[1,2560]{1,0:T(2,128)(2,1)} %refs_1_.1, bf16[1,2560,1024]{2,1,0:T(8,128)(2,1)} %refs_2_.1, bf16[1,2560,128]{2,1,0:T(8,128)(2,1)} %refs_3_.1, ...), custom_call_target="tpu_custom_call" | custom-call | flops 188743680 | bytes 11796480 | tf_op jit(solution)/shard_map/tick/pallas_call | solution.py:328
  18.6 0.7 %store.1 = (bf16[16,2560]{1,0:T(8,128)(2,1)}, bf16[16,128]{1,0:T(8,128)(2,1)}, bf16[16,128]{1,0:T(8,128)(2,1)}) custom-call(bf16[16,2560]{1,0:T(8,128)(2,1)S(1)} %get-tuple-element.9.refs_0_, bf16[16,128]{1,0:T(8,128)(2,1)S(1)} %get-tuple-element.10.refs_1_, bf16[16,128]{1,0:T(8,128)(2,1)S(1)} %get-tuple-element.11.refs_2_), custom_call_target="tpu_custom_call" | custom-call | tf_op jit(solution)/shard_map/store/pallas_call | solution.py:366

commit v6 on v5

--- a/solution.py
+++ b/solution.py
@@ -36,9 +36,7 @@
     nv_out,
     state_v,
     gain_v,
-    normed_v,
     w_v,
-    total_v,
     wo_v,
     qgain_v,
     kgain_v,
@@ -131,6 +129,9 @@
         for h, which in enumerate(chip_order)
     ]
 
+    for copy in projections:
+        copy.start()
+
     barrier = pltpu.get_barrier_semaphore()
     for offset in offsets[:-1]:
         pl.semaphore_signal(
@@ -141,27 +142,38 @@
             barrier, inc=1, device_id=(before, member(offset)), device_id_type=MESH
         )
 
+    lines = (slots // 8 + 1) * 8
+    lane = lax.broadcasted_iota(jnp.int32, (lines, HD), 1)
+    half = HD // 2
+    index = jnp.where(lane < half, lane, lane - half).astype(jnp.float32)
+    frequency = jnp.exp(index * (-2.0 / HD * 13.815510557964274))
+    angles = lax.broadcasted_iota(jnp.int32, (lines, HD), 0).astype(jnp.float32) * frequency
+    unused = jnp.zeros((HD - lines, HD), jnp.float32)
+    sine_table = jnp.sin(angles)
+    sine_table = jnp.where(lane < half, -sine_table, sine_table)
+    cosine_table = jnp.concatenate([jnp.cos(angles), unused], axis=0)
+    sine_table = jnp.concatenate([sine_table, unused], axis=0)
+
     for copy in small[:5]:
         copy.wait()
     hidden = state_v[...].astype(jnp.float32)
     normed = (hidden * inverse_rms(hidden) * gain_v[...].astype(jnp.float32)).astype(jnp.bfloat16)
-    for c in range(CHUNKS):
-        normed_v[c] = normed[:, c * depth : (c + 1) * depth]
-    total_v[...] = jnp.zeros_like(total_v)
 
     on_diagonal = lax.broadcasted_iota(jnp.int32, (rows, rows), 0) == lax.broadcasted_iota(
         jnp.int32, (rows, rows), 1
     )
     spread = jnp.broadcast_to(len_v[...].astype(jnp.float32), (rows, rows))
     position = jnp.sum(jnp.where(on_diagonal, spread, 0.0), axis=1, keepdims=True)
-    lane = lax.broadcasted_iota(jnp.int32, (rows, HD), 1)
-    half = HD // 2
-    index = jnp.where(lane < half, lane, lane - half).astype(jnp.float32)
-    frequency = jnp.exp(index * (-2.0 / HD * 13.815510557964274))
-    angles = position * frequency
-    cosine = jnp.cos(angles)
-    sine = jnp.sin(angles)
-    sine = jnp.where(lane < half, -sine, sine)
+    chosen = (lax.broadcasted_iota(jnp.int32, (rows, HD), 1).astype(jnp.float32) == position).astype(
+        jnp.float32
+    )
+
+    def picked(table):
+        return jnp.dot(
+            chosen, table, precision=lax.Precision.HIGHEST, preferred_element_type=jnp.float32
+        )
+
+    cosine, sine = picked(cosine_table), picked(sine_table)
 
     def rotate(values, cosines, sines):
         return values * cosines + pltpu.roll(values, half, 1) * sines
@@ -179,21 +191,16 @@
     query_gain = qgain_v[...].astype(jnp.float32)
     key_gain = kgain_v[...].astype(jnp.float32)
 
-    def project(c, carry):
+    total = None
+    for c in range(CHUNKS):
         for copy in weights(c):
             copy.wait()
-
-        @pl.when(c == 1)
-        def _():
-            for copy in projections:
-                copy.start()
-
-        span = pl.ds(pl.multiple_of(c * depth, depth), depth)
-        total_v[...] += jnp.dot(normed_v[c], w_v[span, :], preferred_element_type=jnp.float32)
-        return carry
-
-    lax.fori_loop(0, CHUNKS, project, 0)
-    total = total_v[...]
+        term = jnp.dot(
+            normed[:, c * depth : (c + 1) * depth],
+            w_v[c * depth : (c + 1) * depth, :],
+            preferred_element_type=jnp.float32,
+        )
+        total = term if total is None else total + term
 
     key_raw = total[:, query_width : query_width + HD]
     new_value = total[:, query_width + HD :].astype(jnp.bfloat16)
@@ -333,9 +340,7 @@
             scratch_shapes=[
                 pltpu.VMEM((rows, width), jnp.bfloat16),
                 pltpu.VMEM((1, width), jnp.bfloat16),
-                pltpu.VMEM((CHUNKS, rows, width // CHUNKS), jnp.bfloat16),
                 pltpu.VMEM((width, query_width + 2 * HD), jnp.bfloat16),
-                pltpu.VMEM((rows, query_width + 2 * HD), jnp.float32),
                 pltpu.VMEM((chips, query_width, CORES * block), jnp.bfloat16),
                 pltpu.VMEM((1, HD), jnp.bfloat16),
                 pltpu.VMEM((1, HD), jnp.bfloat16),

time: 19.4 us -> 19.7 us (1.015)
  Pallas kernels: 18.6 us -> 18.9 us
    pallas_call x1, Pallas kernels: 18 us -> 18.2 us  [body(): pl.pallas_call(kernel, out_shape=tuple((pltpu.VMEM(shape, jnp.bfloat16) f...]
where the time goes in v6:
time: 19.7 us; the launch traced here: 19.5 us
  Pallas kernels  18.9 us (96%)
  between operations  0.64 us (3%)
    pallas_call x1, Pallas kernels, body(): pl.pallas_call(kernel, out_shape=tuple((pltpu.VMEM(shape, jnp.bfloat16) f...  18.2 us
    pallas_call x1, Pallas kernels, body(): pl.pallas_call(store_kernel, out_shape=tuple((pltpu.HBM(shape, jnp.bfloat...  0.67 us

profile of v6, /device:TPU:0, one launch (start us, length us, event | category | flops | bytes accessed | tf_op | source)
XLA Modules:
  0.0 19.5 jit_solution(15594470965992149627)
XLA Ops:
  0.6 18.2 %tick.1 = (bf16[16,2560]{1,0:T(8,128)(2,1)S(1)}, bf16[16,128]{1,0:T(8,128)(2,1)S(1)}, bf16[16,128]{1,0:T(8,128)(2,1)S(1)}) custom-call(bf16[1,16,2560]{2,1,0:T(8,128)(2,1)} %refs_0_.1, bf16[1,2560]{1,0:T(2,128)(2,1)} %refs_1_.1, bf16[1,2560,1024]{2,1,0:T(8,128)(2,1)} %refs_2_.1, bf16[1,2560,128]{2,1,0:T(8,128)(2,1)} %refs_3_.1, ...), custom_call_target="tpu_custom_call" | custom-call | flops 188743680 | bytes 11796480 | tf_op jit(solution)/shard_map/tick/pallas_call | solution.py:335
  18.8 0.7 %store.1 = (bf16[16,2560]{1,0:T(8,128)(2,1)}, bf16[16,128]{1,0:T(8,128)(2,1)}, bf16[16,128]{1,0:T(8,128)(2,1)}) custom-call(bf16[16,2560]{1,0:T(8,128)(2,1)S(1)} %get-tuple-element.9.refs_0_, bf16[16,128]{1,0:T(8,128)(2,1)S(1)} %get-tuple-element.10.refs_1_, bf16[16,128]{1,0:T(8,128)(2,1)S(1)} %get-tuple-element.11.refs_2_), custom_call_target="tpu_custom_call" | custom-call | tf_op jit(solution)/shard_map/store/pallas_call | solution.py:371
